TPU v7x, 256 devices: a whole 4x4x8 slice. The times are simulated.
256 devices in a mesh: ctx: 32 (over z, y_lo, core), tr: 2 (over y_hi), tc: 4 (over x).
Axes of the slice: x: 4, y: 4 (y_hi: 2, y_lo: 2; y = y_hi * 2 + y_lo), z: 8, core: 2. Of those that a mesh axis runs over, the one named last changes fastest.
Arguments:
- hidden: bfloat16 [16384, 4096], P(('ctx', 'tc'), 'tr'), may hold values from -6 to 6
- norm_gain: float32 [4096], P('tr'), may hold values from 0.25 to 1.75
- seg_lengths: int32 [64], replicated, may hold values from 1 to 512, 16384 in all
- q_weight: bfloat16 [4096, 2048], P('tr', 'tc'), may hold values from -3 to 3
- key_matrix: bfloat16 [4096, 512], P('tr', 'tc'), may hold values from -3 to 3
- value_matrix: bfloat16 [4096, 512], P('tr', 'tc'), may hold values from -0.09375 to 0.09375
- o_weight: bfloat16 [2048, 4096], P('tc', 'tr'), may hold values from -0.125 to 0.125
Outputs:
- layer_out: bfloat16 [16384, 4096], P(('ctx', 'tc'), 'tr')
Inputs may be any that keep to these rules, and one draw needn't show every extreme that they name: `seg_lengths`: entry 0 is the length of the shared prefix, the other entries the candidates' lengths in list order; all sum to 16384, and the longest is exactly 512.
All inputs are finite; a program needn't handle non-finite values.
Results may differ from a plain program's by a relative error of at most 0.01.
Values may be sent and summed in bfloat16 or wider, within the bound.
No kernel may reach another device: no remote copies, remote signals or barrier semaphores. Data moves between devices by JAX's collectives and lax.ppermute only.
A program may use at most 64 MiB of HBM per device.

v0:
```python
import jax
import jax.numpy as jnp
from jax import lax
from jax.sharding import PartitionSpec as P

D = 4096
HEAD_SIZE = 128
epsilon = 1e-05
rope_base = 500000.0
masked_score = -1e30


def from_behind(block, axis, distance):
    devices = range(lax.axis_size(axis))
    route = [(i - distance, i) for i in devices if i - distance in devices]
    return lax.ppermute(block, axis, route)


def rotate(heads_data, positions):
    half_dim = heads_data.shape[-1] // 2
    frequency = rope_base ** (
        -(jnp.arange(half_dim, dtype=jnp.float32) * 2.0 / heads_data.shape[-1])
    )
    angles = positions.astype(jnp.float32)[:, None] * frequency[None, :]
    cosine = jnp.cos(angles)[:, None, :]
    sine_part = jnp.sin(angles)[:, None, :]
    first = heads_data[..., :half_dim]
    second = heads_data[..., half_dim:]
    return jnp.concatenate(
        [first * cosine - second * sine_part, second * cosine + first * sine_part], axis=-1
    )


def segment_of(positions, seg_lengths):
    bounds = jnp.cumsum(seg_lengths)[:-1]
    return jnp.sum((positions[:, None] >= bounds[None, :]).astype(jnp.int32), axis=1)


def per_device(hidden, norm_gain, seg_lengths, q_weight, key_matrix, value_matrix, o_weight):
    wide_hidden = hidden.astype(jnp.float32)
    squares = lax.psum(jnp.sum(wide_hidden * wide_hidden, axis=1), "tr")
    normed_local = (wide_hidden * lax.rsqrt(squares[:, None] / D + epsilon) * norm_gain).astype(
        jnp.bfloat16
    )
    normalized_rows = lax.all_gather(normed_local, "tc", axis=0, tiled=True)
    rows_per_block = normalized_rows.shape[0]
    query_rows = rows_per_block // lax.axis_size("tr")
    query_width = q_weight.shape[1]
    key_width = key_matrix.shape[1]
    summed = lax.psum_scatter(
        jnp.concatenate(
            [
                jnp.dot(normalized_rows, q_weight, preferred_element_type=jnp.float32),
                jnp.dot(normalized_rows, key_matrix, preferred_element_type=jnp.float32),
                jnp.dot(normalized_rows, value_matrix, preferred_element_type=jnp.float32),
            ],
            axis=1,
        ),
        "tr",
        scatter_dimension=0,
        tiled=True,
    )
    cycle_index = lax.axis_index("ctx")
    cycle_size = lax.axis_size("ctx")
    query_pos = (
        cycle_index * rows_per_block
        + lax.axis_index("tr") * query_rows
        + jnp.arange(query_rows, dtype=jnp.int32)
    )
    head_local = query_width // HEAD_SIZE
    key_heads = key_width // HEAD_SIZE
    head_groups = head_local // key_heads
    queries = rotate(summed[:, :query_width].reshape(query_rows, head_local, HEAD_SIZE), query_pos)
    queries = queries.astype(jnp.bfloat16).reshape(query_rows, key_heads, head_groups, HEAD_SIZE)
    key_block_list = rotate(
        summed[:, query_width : query_width + key_width].reshape(query_rows, key_heads, HEAD_SIZE),
        query_pos,
    )
    key_block_list = key_block_list.astype(jnp.bfloat16)
    value_block_list = summed[:, query_width + key_width :].astype(jnp.bfloat16)
    local_pairs = jnp.concatenate(
        [key_block_list.reshape(query_rows, key_width), value_block_list], axis=1
    )
    query_seg = segment_of(query_pos, seg_lengths)
    score_scale = HEAD_SIZE ** (-0.5)

    def attend(softmax_state, key_block, source):
        running_max, weight_sum, accumulated = softmax_state
        key_pos = source * rows_per_block + jnp.arange(rows_per_block, dtype=jnp.int32)
        key_seg = segment_of(key_pos, seg_lengths)
        visible = (key_pos[None, :] <= query_pos[:, None]) & (
            (key_seg[None, :] == 0) | (key_seg[None, :] == query_seg[:, None])
        )
        block_keys = key_block[:, :key_width].reshape(rows_per_block, key_heads, HEAD_SIZE)
        block_values = key_block[:, key_width:].reshape(rows_per_block, key_heads, HEAD_SIZE)
        scores = (
            jnp.einsum("qhgd,khd->hgqk", queries, block_keys, preferred_element_type=jnp.float32)
            * score_scale
        )
        scores = jnp.where(visible, scores, masked_score)
        new_max = jnp.maximum(running_max, jnp.max(scores, axis=-1))
        factor = jnp.exp(running_max - new_max)
        weights = jnp.where(visible, jnp.exp(scores - new_max[..., None]), 0.0)
        weight_sum = weight_sum * factor + jnp.sum(weights, axis=-1)
        accumulated = accumulated * factor[..., None] + jnp.einsum(
            "hgqk,khd->hgqd",
            weights.astype(jnp.bfloat16),
            block_values,
            preferred_element_type=jnp.float32,
        )
        return (new_max, weight_sum, accumulated)

    def maybe_attend(softmax_state, key_block, step_number):
        source = (cycle_index - step_number) % cycle_size
        needed = step_number <= cycle_index
        return lax.cond(
            needed,
            lambda current: attend(current, key_block, source),
            lambda current: current,
            softmax_state,
        )

    state_shape = (key_heads, head_groups, query_rows)
    softmax_state = (
        jnp.full(state_shape, masked_score, jnp.float32),
        jnp.zeros(state_shape, jnp.float32),
        jnp.zeros(state_shape + (HEAD_SIZE,), jnp.float32),
    )
    key_block = lax.all_gather(local_pairs, "tr", axis=0, tiled=True)
    softmax_state = maybe_attend(softmax_state, key_block, 0)

    def advance(step_number, loop_carry):
        moving, current = loop_carry
        moving = from_behind(moving, "ctx", 1)
        return (moving, maybe_attend(current, moving, step_number))

    key_block, softmax_state = lax.fori_loop(1, cycle_size, advance, (key_block, softmax_state))
    running_max, weight_sum, accumulated = softmax_state
    mixed = accumulated / weight_sum[..., None]
    attended = (
        jnp.transpose(mixed, (2, 0, 1, 3)).reshape(query_rows, query_width).astype(jnp.bfloat16)
    )
    partial_terms = jnp.dot(
        lax.all_gather(attended, "tr", axis=0, tiled=True),
        o_weight,
        preferred_element_type=jnp.float32,
    )
    summed_out = lax.psum_scatter(
        partial_terms.astype(jnp.bfloat16), "tc", scatter_dimension=0, tiled=True
    ).astype(jnp.float32)
    return (wide_hidden + summed_out).astype(jnp.bfloat16)


def solution(mesh):
    in_specs = (
        P(("ctx", "tc"), "tr"),
        P("tr"),
        P(),
        P("tr", "tc"),
        P("tr", "tc"),
        P("tr", "tc"),
        P("tc", "tr"),
    )
    out_specs = P(("ctx", "tc"), "tr")
    return jax.shard_map(
        per_device, mesh=mesh, in_specs=in_specs, out_specs=out_specs, check_vma=False
    )
```

profile of v0, /device:TPU:1, one launch (start us, length us, event | category | flops | bytes accessed | tf_op | source)
XLA Modules:
  0.0 513.1 jit_solution(15915280285968883886)
XLA Ops:
  7.9 6.0 %psum.7 = f32[128]{0:T(128)S(1)} all-reduce(f32[128]{0:T(128)S(1)} %fusion.40), channel_id=1, replica_groups=mesh['ctx'=32,'tr'=2,'tc'=4] {'tr'}, use_global_device_ids=true, to_apply=%region_1.0 | all-reduce | flops 128 | bytes 1024 | tf_op jit(solution)/shard_map/psum | solution.py:41
  16.1 37.7 %all-gather.2.cloned.1.call-done = bf16[512,2048]{1,0:T(8,128)(2,1)} async-done(((bf16[128,2048]{1,0:T(8,128)(2,1)}), bf16[512,2048]{1,0:T(8,128)(2,1)}) %all-gather.2.cloned.1.call-update) | async-done | bytes 2097168 | tf_op jit(solution)/shard_map/all_gather | solution.py:45
  62.3 31.2 %reduce-scatter.3.cloned.1.call-done = f32[256,768]{0,1:T(8,128)} async-done(((f32[512,768]{0,1:T(8,128)}), f32[256,768]{0,1:T(8,128)}) %reduce-scatter.3.cloned.1.call-update) | async-done | bytes 786448 | tf_op jit(solution)/shard_map/reduce_scatter | solution.py:50
  100.3 6.5 %all_gather.10 = bf16[512,256]{0,1:T(8,128)(2,1)S(1)} all-gather(bf16[256,256]{0,1:T(8,128)(2,1)S(1)} %pad_maximum_fusion.2), channel_id=1, replica_groups=mesh['ctx'=32,'tr'=2,'tc'=4] {'tr'}, dimensions={0}, use_global_device_ids=true | all-gather | bytes 393216 | tf_op jit(solution)/shard_map/all_gather | solution.py:129
  113.1 279.2 %while.22 = (s32[]{:T(128)}, bf16[512,256]{1,0:T(8,128)(2,1)S(1)}, f32[1,4,256]{2,1,0:T(4,128)S(1)}, f32[1,4,256]{2,1,0:T(4,128)S(1)}, f32[1,4,256,128]{3,2,1,0:...) while((s32[]{:T(128)}, bf16[512,256]{1,0:T(8,128)(2,1)S(1)}, ...), condition=%wide.region_18.19_spmd.clone, body=%wide.region_11.18_spmd.clone.sunk | while | flops 276142272 | bytes 10047672 | solution.py:137
  130.5 7.1 %collective-permute-start = (bf16[512,256]{1,0:T(8,128)(2,1)S(1)}, bf16[512,256]{1,0:T(8,128)(2,1)S(1)}, u32[]{:S(2)}, u32[]{:S(2)}) collective-permute-start(bf16[512,256]{1,0:T(8,128)(2,1)S(1)} %get-tuple-element.707), channel_id=1, source_target_pairs={{0,8},{8,16},{16,24},{24,32},{32,40},{40,48},{48,56},{56,64},{64,7... | collective-permute-start | bytes 786440 | tf_op jit(solution)/shard_map/while/body/eval_jaxpr/ppermute | solution.py:16
  164.9 8.0 %collective-permute-start = (bf16[512,256]{1,0:T(8,128)(2,1)S(1)}, bf16[512,256]{1,0:T(8,128)(2,1)S(1)}, u32[]{:S(2)}, u32[]{:S(2)}) collective-permute-start(bf16[512,256]{1,0:T(8,128)(2,1)S(1)} %get-tuple-element.707), channel_id=1, source_target_pairs={{0,8},{8,16},{16,24},{24,32},{32,40},{40,48},{48,56},{56,64},{64,7... | collective-permute-start | bytes 786440 | tf_op jit(solution)/shard_map/while/body/eval_jaxpr/ppermute | solution.py:16
  176.2 5.3 %collective-permute-start = (bf16[512,256]{1,0:T(8,128)(2,1)S(1)}, bf16[512,256]{1,0:T(8,128)(2,1)S(1)}, u32[]{:S(2)}, u32[]{:S(2)}) collective-permute-start(bf16[512,256]{1,0:T(8,128)(2,1)S(1)} %get-tuple-element.707), channel_id=1, source_target_pairs={{0,8},{8,16},{16,24},{24,32},{32,40},{40,48},{48,56},{56,64},{64,7... | collective-permute-start | bytes 786440 | tf_op jit(solution)/shard_map/while/body/eval_jaxpr/ppermute | solution.py:16
  193.4 5.3 %collective-permute-start = (bf16[512,256]{1,0:T(8,128)(2,1)S(1)}, bf16[512,256]{1,0:T(8,128)(2,1)S(1)}, u32[]{:S(2)}, u32[]{:S(2)}) collective-permute-start(bf16[512,256]{1,0:T(8,128)(2,1)S(1)} %get-tuple-element.707), channel_id=1, source_target_pairs={{0,8},{8,16},{16,24},{24,32},{32,40},{40,48},{48,56},{56,64},{64,7... | collective-permute-start | bytes 786440 | tf_op jit(solution)/shard_map/while/body/eval_jaxpr/ppermute | solution.py:16
  202.1 5.3 %collective-permute-start = (bf16[512,256]{1,0:T(8,128)(2,1)S(1)}, bf16[512,256]{1,0:T(8,128)(2,1)S(1)}, u32[]{:S(2)}, u32[]{:S(2)}) collective-permute-start(bf16[512,256]{1,0:T(8,128)(2,1)S(1)} %get-tuple-element.707), channel_id=1, source_target_pairs={{0,8},{8,16},{16,24},{24,32},{32,40},{40,48},{48,56},{56,64},{64,7... | collective-permute-start | bytes 786440 | tf_op jit(solution)/shard_map/while/body/eval_jaxpr/ppermute | solution.py:16
  219.3 5.3 %collective-permute-start = (bf16[512,256]{1,0:T(8,128)(2,1)S(1)}, bf16[512,256]{1,0:T(8,128)(2,1)S(1)}, u32[]{:S(2)}, u32[]{:S(2)}) collective-permute-start(bf16[512,256]{1,0:T(8,128)(2,1)S(1)} %get-tuple-element.707), channel_id=1, source_target_pairs={{0,8},{8,16},{16,24},{24,32},{32,40},{40,48},{48,56},{56,64},{64,7... | collective-permute-start | bytes 786440 | tf_op jit(solution)/shard_map/while/body/eval_jaxpr/ppermute | solution.py:16
  228.0 5.3 %collective-permute-start = (bf16[512,256]{1,0:T(8,128)(2,1)S(1)}, bf16[512,256]{1,0:T(8,128)(2,1)S(1)}, u32[]{:S(2)}, u32[]{:S(2)}) collective-permute-start(bf16[512,256]{1,0:T(8,128)(2,1)S(1)} %get-tuple-element.707), channel_id=1, source_target_pairs={{0,8},{8,16},{16,24},{24,32},{32,40},{40,48},{48,56},{56,64},{64,7... | collective-permute-start | bytes 786440 | tf_op jit(solution)/shard_map/while/body/eval_jaxpr/ppermute | solution.py:16
  236.6 5.3 %collective-permute-start = (bf16[512,256]{1,0:T(8,128)(2,1)S(1)}, bf16[512,256]{1,0:T(8,128)(2,1)S(1)}, u32[]{:S(2)}, u32[]{:S(2)}) collective-permute-start(bf16[512,256]{1,0:T(8,128)(2,1)S(1)} %get-tuple-element.707), channel_id=1, source_target_pairs={{0,8},{8,16},{16,24},{24,32},{32,40},{40,48},{48,56},{56,64},{64,7... | collective-permute-start | bytes 786440 | tf_op jit(solution)/shard_map/while/body/eval_jaxpr/ppermute | solution.py:16
  245.2 5.3 %collective-permute-start = (bf16[512,256]{1,0:T(8,128)(2,1)S(1)}, bf16[512,256]{1,0:T(8,128)(2,1)S(1)}, u32[]{:S(2)}, u32[]{:S(2)}) collective-permute-start(bf16[512,256]{1,0:T(8,128)(2,1)S(1)} %get-tuple-element.707), channel_id=1, source_target_pairs={{0,8},{8,16},{16,24},{24,32},{32,40},{40,48},{48,56},{56,64},{64,7... | collective-permute-start | bytes 786440 | tf_op jit(solution)/shard_map/while/body/eval_jaxpr/ppermute | solution.py:16
  262.5 5.3 %collective-permute-start = (bf16[512,256]{1,0:T(8,128)(2,1)S(1)}, bf16[512,256]{1,0:T(8,128)(2,1)S(1)}, u32[]{:S(2)}, u32[]{:S(2)}) collective-permute-start(bf16[512,256]{1,0:T(8,128)(2,1)S(1)} %get-tuple-element.707), channel_id=1, source_target_pairs={{0,8},{8,16},{16,24},{24,32},{32,40},{40,48},{48,56},{56,64},{64,7... | collective-permute-start | bytes 786440 | tf_op jit(solution)/shard_map/while/body/eval_jaxpr/ppermute | solution.py:16
  271.1 5.3 %collective-permute-start = (bf16[512,256]{1,0:T(8,128)(2,1)S(1)}, bf16[512,256]{1,0:T(8,128)(2,1)S(1)}, u32[]{:S(2)}, u32[]{:S(2)}) collective-permute-start(bf16[512,256]{1,0:T(8,128)(2,1)S(1)} %get-tuple-element.707), channel_id=1, source_target_pairs={{0,8},{8,16},{16,24},{24,32},{32,40},{40,48},{48,56},{56,64},{64,7... | collective-permute-start | bytes 786440 | tf_op jit(solution)/shard_map/while/body/eval_jaxpr/ppermute | solution.py:16
  288.4 5.3 %collective-permute-start = (bf16[512,256]{1,0:T(8,128)(2,1)S(1)}, bf16[512,256]{1,0:T(8,128)(2,1)S(1)}, u32[]{:S(2)}, u32[]{:S(2)}) collective-permute-start(bf16[512,256]{1,0:T(8,128)(2,1)S(1)} %get-tuple-element.707), channel_id=1, source_target_pairs={{0,8},{8,16},{16,24},{24,32},{32,40},{40,48},{48,56},{56,64},{64,7... | collective-permute-start | bytes 786440 | tf_op jit(solution)/shard_map/while/body/eval_jaxpr/ppermute | solution.py:16
  297.0 5.3 %collective-permute-start = (bf16[512,256]{1,0:T(8,128)(2,1)S(1)}, bf16[512,256]{1,0:T(8,128)(2,1)S(1)}, u32[]{:S(2)}, u32[]{:S(2)}) collective-permute-start(bf16[512,256]{1,0:T(8,128)(2,1)S(1)} %get-tuple-element.707), channel_id=1, source_target_pairs={{0,8},{8,16},{16,24},{24,32},{32,40},{40,48},{48,56},{56,64},{64,7... | collective-permute-start | bytes 786440 | tf_op jit(solution)/shard_map/while/body/eval_jaxpr/ppermute | solution.py:16
  314.3 5.3 %collective-permute-start = (bf16[512,256]{1,0:T(8,128)(2,1)S(1)}, bf16[512,256]{1,0:T(8,128)(2,1)S(1)}, u32[]{:S(2)}, u32[]{:S(2)}) collective-permute-start(bf16[512,256]{1,0:T(8,128)(2,1)S(1)} %get-tuple-element.707), channel_id=1, source_target_pairs={{0,8},{8,16},{16,24},{24,32},{32,40},{40,48},{48,56},{56,64},{64,7... | collective-permute-start | bytes 786440 | tf_op jit(solution)/shard_map/while/body/eval_jaxpr/ppermute | solution.py:16
  357.4 9.1 %collective-permute-start = (bf16[512,256]{1,0:T(8,128)(2,1)S(1)}, bf16[512,256]{1,0:T(8,128)(2,1)S(1)}, u32[]{:S(2)}, u32[]{:S(2)}) collective-permute-start(bf16[512,256]{1,0:T(8,128)(2,1)S(1)} %get-tuple-element.707), channel_id=1, source_target_pairs={{0,8},{8,16},{16,24},{24,32},{32,40},{40,48},{48,56},{56,64},{64,7... | collective-permute-start | bytes 786440 | tf_op jit(solution)/shard_map/while/body/eval_jaxpr/ppermute | solution.py:16
  369.9 6.5 %collective-permute-start = (bf16[512,256]{1,0:T(8,128)(2,1)S(1)}, bf16[512,256]{1,0:T(8,128)(2,1)S(1)}, u32[]{:S(2)}, u32[]{:S(2)}) collective-permute-start(bf16[512,256]{1,0:T(8,128)(2,1)S(1)} %get-tuple-element.707), channel_id=1, source_target_pairs={{0,8},{8,16},{16,24},{24,32},{32,40},{40,48},{48,56},{56,64},{64,7... | collective-permute-start | bytes 786440 | tf_op jit(solution)/shard_map/while/body/eval_jaxpr/ppermute | solution.py:16
  379.7 9.2 %collective-permute-start = (bf16[512,256]{1,0:T(8,128)(2,1)S(1)}, bf16[512,256]{1,0:T(8,128)(2,1)S(1)}, u32[]{:S(2)}, u32[]{:S(2)}) collective-permute-start(bf16[512,256]{1,0:T(8,128)(2,1)S(1)} %get-tuple-element.707), channel_id=1, source_target_pairs={{0,8},{8,16},{16,24},{24,32},{32,40},{40,48},{48,56},{56,64},{64,7... | collective-permute-start | bytes 786440 | tf_op jit(solution)/shard_map/while/body/eval_jaxpr/ppermute | solution.py:16
  392.5 7.4 %all_gather.11 = bf16[512,512]{0,1:T(8,128)(2,1)S(1)} all-gather(bf16[256,512]{0,1:T(8,128)(2,1)S(1)} %bitcast.110), channel_id=1, replica_groups=mesh['ctx'=32,'tr'=2,'tc'=4] {'tr'}, dimensions={0}, use_global_device_ids=true | all-gather | bytes 786432 | tf_op jit(solution)/shard_map/all_gather | solution.py:144
  402.5 102.1 %reduce-scatter.5.cloned.1.call-done = bf16[128,2048]{1,0:T(8,128)(2,1)} async-done(((bf16[512,2048]{1,0:T(8,128)(2,1)}), bf16[128,2048]{1,0:T(8,128)(2,1)}) %reduce-scatter.5.cloned.1.call-update) | async-done | bytes 524304 | tf_op jit(solution)/shard_map/reduce_scatter | solution.py:148
  (220 shorter events, 211.0 us)
Async XLA Ops:
  6.5 47.2 %all-gather.2.cloned.1.call-start = ((), (), s32[]{:S(2)}) async-start(), calls=%async_computation.2 | async-start | bytes 2621440 | tf_op jit(solution)/shard_map/all_gather | solution.py:45
  16.0 77.5 %reduce-scatter.3.cloned.1.call-start = ((), (), s32[]{:S(2)}) async-start(), calls=%async_computation.3 | async-start | bytes 2359296 | tf_op jit(solution)/shard_map/reduce_scatter | solution.py:50
  60.6 444.0 %reduce-scatter.5.cloned.1.call-start = ((), (), s32[]{:S(2)}) async-start(), calls=%async_computation.4 | async-start | bytes 2621440 | tf_op jit(solution)/shard_map/reduce_scatter | solution.py:148
  130.5 10.4 %collective-permute-start = (bf16[512,256]{1,0:T(8,128)(2,1)S(1)}, bf16[512,256]{1,0:T(8,128)(2,1)S(1)}, u32[]{:S(2)}, u32[]{:S(2)}) collective-permute-start(bf16[512,256]{1,0:T(8,128)(2,1)S(1)} %get-tuple-element.707), channel_id=1, source_target_pairs={{0,8},{8,16},{16,24},{24,32},{32,40},{40,48},{48,56},{56,64},{64,7... | collective-permute-start | bytes 786440 | tf_op jit(solution)/shard_map/while/body/eval_jaxpr/ppermute | solution.py:16
  164.9 11.3 %collective-permute-start = (bf16[512,256]{1,0:T(8,128)(2,1)S(1)}, bf16[512,256]{1,0:T(8,128)(2,1)S(1)}, u32[]{:S(2)}, u32[]{:S(2)}) collective-permute-start(bf16[512,256]{1,0:T(8,128)(2,1)S(1)} %get-tuple-element.707), channel_id=1, source_target_pairs={{0,8},{8,16},{16,24},{24,32},{32,40},{40,48},{48,56},{56,64},{64,7... | collective-permute-start | bytes 786440 | tf_op jit(solution)/shard_map/while/body/eval_jaxpr/ppermute | solution.py:16
  176.2 8.6 %collective-permute-start = (bf16[512,256]{1,0:T(8,128)(2,1)S(1)}, bf16[512,256]{1,0:T(8,128)(2,1)S(1)}, u32[]{:S(2)}, u32[]{:S(2)}) collective-permute-start(bf16[512,256]{1,0:T(8,128)(2,1)S(1)} %get-tuple-element.707), channel_id=1, source_target_pairs={{0,8},{8,16},{16,24},{24,32},{32,40},{40,48},{48,56},{56,64},{64,7... | collective-permute-start | bytes 786440 | tf_op jit(solution)/shard_map/while/body/eval_jaxpr/ppermute | solution.py:16
  184.8 8.6 %collective-permute-start = (bf16[512,256]{1,0:T(8,128)(2,1)S(1)}, bf16[512,256]{1,0:T(8,128)(2,1)S(1)}, u32[]{:S(2)}, u32[]{:S(2)}) collective-permute-start(bf16[512,256]{1,0:T(8,128)(2,1)S(1)} %get-tuple-element.707), channel_id=1, source_target_pairs={{0,8},{8,16},{16,24},{24,32},{32,40},{40,48},{48,56},{56,64},{64,7... | collective-permute-start | bytes 786440 | tf_op jit(solution)/shard_map/while/body/eval_jaxpr/ppermute | solution.py:16
  193.4 8.6 %collective-permute-start = (bf16[512,256]{1,0:T(8,128)(2,1)S(1)}, bf16[512,256]{1,0:T(8,128)(2,1)S(1)}, u32[]{:S(2)}, u32[]{:S(2)}) collective-permute-start(bf16[512,256]{1,0:T(8,128)(2,1)S(1)} %get-tuple-element.707), channel_id=1, source_target_pairs={{0,8},{8,16},{16,24},{24,32},{32,40},{40,48},{48,56},{56,64},{64,7... | collective-permute-start | bytes 786440 | tf_op jit(solution)/shard_map/while/body/eval_jaxpr/ppermute | solution.py:16
  202.1 8.6 %collective-permute-start = (bf16[512,256]{1,0:T(8,128)(2,1)S(1)}, bf16[512,256]{1,0:T(8,128)(2,1)S(1)}, u32[]{:S(2)}, u32[]{:S(2)}) collective-permute-start(bf16[512,256]{1,0:T(8,128)(2,1)S(1)} %get-tuple-element.707), channel_id=1, source_target_pairs={{0,8},{8,16},{16,24},{24,32},{32,40},{40,48},{48,56},{56,64},{64,7... | collective-permute-start | bytes 786440 | tf_op jit(solution)/shard_map/while/body/eval_jaxpr/ppermute | solution.py:16
  210.7 8.6 %collective-permute-start = (bf16[512,256]{1,0:T(8,128)(2,1)S(1)}, bf16[512,256]{1,0:T(8,128)(2,1)S(1)}, u32[]{:S(2)}, u32[]{:S(2)}) collective-permute-start(bf16[512,256]{1,0:T(8,128)(2,1)S(1)} %get-tuple-element.707), channel_id=1, source_target_pairs={{0,8},{8,16},{16,24},{24,32},{32,40},{40,48},{48,56},{56,64},{64,7... | collective-permute-start | bytes 786440 | tf_op jit(solution)/shard_map/while/body/eval_jaxpr/ppermute | solution.py:16
  219.3 8.6 %collective-permute-start = (bf16[512,256]{1,0:T(8,128)(2,1)S(1)}, bf16[512,256]{1,0:T(8,128)(2,1)S(1)}, u32[]{:S(2)}, u32[]{:S(2)}) collective-permute-start(bf16[512,256]{1,0:T(8,128)(2,1)S(1)} %get-tuple-element.707), channel_id=1, source_target_pairs={{0,8},{8,16},{16,24},{24,32},{32,40},{40,48},{48,56},{56,64},{64,7... | collective-permute-start | bytes 786440 | tf_op jit(solution)/shard_map/while/body/eval_jaxpr/ppermute | solution.py:16
  228.0 8.6 %collective-permute-start = (bf16[512,256]{1,0:T(8,128)(2,1)S(1)}, bf16[512,256]{1,0:T(8,128)(2,1)S(1)}, u32[]{:S(2)}, u32[]{:S(2)}) collective-permute-start(bf16[512,256]{1,0:T(8,128)(2,1)S(1)} %get-tuple-element.707), channel_id=1, source_target_pairs={{0,8},{8,16},{16,24},{24,32},{32,40},{40,48},{48,56},{56,64},{64,7... | collective-permute-start | bytes 786440 | tf_op jit(solution)/shard_map/while/body/eval_jaxpr/ppermute | solution.py:16
  236.6 8.6 %collective-permute-start = (bf16[512,256]{1,0:T(8,128)(2,1)S(1)}, bf16[512,256]{1,0:T(8,128)(2,1)S(1)}, u32[]{:S(2)}, u32[]{:S(2)}) collective-permute-start(bf16[512,256]{1,0:T(8,128)(2,1)S(1)} %get-tuple-element.707), channel_id=1, source_target_pairs={{0,8},{8,16},{16,24},{24,32},{32,40},{40,48},{48,56},{56,64},{64,7... | collective-permute-start | bytes 786440 | tf_op jit(solution)/shard_map/while/body/eval_jaxpr/ppermute | solution.py:16
  245.2 8.6 %collective-permute-start = (bf16[512,256]{1,0:T(8,128)(2,1)S(1)}, bf16[512,256]{1,0:T(8,128)(2,1)S(1)}, u32[]{:S(2)}, u32[]{:S(2)}) collective-permute-start(bf16[512,256]{1,0:T(8,128)(2,1)S(1)} %get-tuple-element.707), channel_id=1, source_target_pairs={{0,8},{8,16},{16,24},{24,32},{32,40},{40,48},{48,56},{56,64},{64,7... | collective-permute-start | bytes 786440 | tf_op jit(solution)/shard_map/while/body/eval_jaxpr/ppermute | solution.py:16
  253.8 8.6 %collective-permute-start = (bf16[512,256]{1,0:T(8,128)(2,1)S(1)}, bf16[512,256]{1,0:T(8,128)(2,1)S(1)}, u32[]{:S(2)}, u32[]{:S(2)}) collective-permute-start(bf16[512,256]{1,0:T(8,128)(2,1)S(1)} %get-tuple-element.707), channel_id=1, source_target_pairs={{0,8},{8,16},{16,24},{24,32},{32,40},{40,48},{48,56},{56,64},{64,7... | collective-permute-start | bytes 786440 | tf_op jit(solution)/shard_map/while/body/eval_jaxpr/ppermute | solution.py:16
  262.5 8.6 %collective-permute-start = (bf16[512,256]{1,0:T(8,128)(2,1)S(1)}, bf16[512,256]{1,0:T(8,128)(2,1)S(1)}, u32[]{:S(2)}, u32[]{:S(2)}) collective-permute-start(bf16[512,256]{1,0:T(8,128)(2,1)S(1)} %get-tuple-element.707), channel_id=1, source_target_pairs={{0,8},{8,16},{16,24},{24,32},{32,40},{40,48},{48,56},{56,64},{64,7... | collective-permute-start | bytes 786440 | tf_op jit(solution)/shard_map/while/body/eval_jaxpr/ppermute | solution.py:16
  271.1 8.6 %collective-permute-start = (bf16[512,256]{1,0:T(8,128)(2,1)S(1)}, bf16[512,256]{1,0:T(8,128)(2,1)S(1)}, u32[]{:S(2)}, u32[]{:S(2)}) collective-permute-start(bf16[512,256]{1,0:T(8,128)(2,1)S(1)} %get-tuple-element.707), channel_id=1, source_target_pairs={{0,8},{8,16},{16,24},{24,32},{32,40},{40,48},{48,56},{56,64},{64,7... | collective-permute-start | bytes 786440 | tf_op jit(solution)/shard_map/while/body/eval_jaxpr/ppermute | solution.py:16
  279.7 8.6 %collective-permute-start = (bf16[512,256]{1,0:T(8,128)(2,1)S(1)}, bf16[512,256]{1,0:T(8,128)(2,1)S(1)}, u32[]{:S(2)}, u32[]{:S(2)}) collective-permute-start(bf16[512,256]{1,0:T(8,128)(2,1)S(1)} %get-tuple-element.707), channel_id=1, source_target_pairs={{0,8},{8,16},{16,24},{24,32},{32,40},{40,48},{48,56},{56,64},{64,7... | collective-permute-start | bytes 786440 | tf_op jit(solution)/shard_map/while/body/eval_jaxpr/ppermute | solution.py:16
  288.4 8.6 %collective-permute-start = (bf16[512,256]{1,0:T(8,128)(2,1)S(1)}, bf16[512,256]{1,0:T(8,128)(2,1)S(1)}, u32[]{:S(2)}, u32[]{:S(2)}) collective-permute-start(bf16[512,256]{1,0:T(8,128)(2,1)S(1)} %get-tuple-element.707), channel_id=1, source_target_pairs={{0,8},{8,16},{16,24},{24,32},{32,40},{40,48},{48,56},{56,64},{64,7... | collective-permute-start | bytes 786440 | tf_op jit(solution)/shard_map/while/body/eval_jaxpr/ppermute | solution.py:16
  297.0 8.6 %collective-permute-start = (bf16[512,256]{1,0:T(8,128)(2,1)S(1)}, bf16[512,256]{1,0:T(8,128)(2,1)S(1)}, u32[]{:S(2)}, u32[]{:S(2)}) collective-permute-start(bf16[512,256]{1,0:T(8,128)(2,1)S(1)} %get-tuple-element.707), channel_id=1, source_target_pairs={{0,8},{8,16},{16,24},{24,32},{32,40},{40,48},{48,56},{56,64},{64,7... | collective-permute-start | bytes 786440 | tf_op jit(solution)/shard_map/while/body/eval_jaxpr/ppermute | solution.py:16
  331.5 8.6 %collective-permute-start = (bf16[512,256]{1,0:T(8,128)(2,1)S(1)}, bf16[512,256]{1,0:T(8,128)(2,1)S(1)}, u32[]{:S(2)}, u32[]{:S(2)}) collective-permute-start(bf16[512,256]{1,0:T(8,128)(2,1)S(1)} %get-tuple-element.707), channel_id=1, source_target_pairs={{0,8},{8,16},{16,24},{24,32},{32,40},{40,48},{48,56},{56,64},{64,7... | collective-permute-start | bytes 786440 | tf_op jit(solution)/shard_map/while/body/eval_jaxpr/ppermute | solution.py:16
  357.4 12.4 %collective-permute-start = (bf16[512,256]{1,0:T(8,128)(2,1)S(1)}, bf16[512,256]{1,0:T(8,128)(2,1)S(1)}, u32[]{:S(2)}, u32[]{:S(2)}) collective-permute-start(bf16[512,256]{1,0:T(8,128)(2,1)S(1)} %get-tuple-element.707), channel_id=1, source_target_pairs={{0,8},{8,16},{16,24},{24,32},{32,40},{40,48},{48,56},{56,64},{64,7... | collective-permute-start | bytes 786440 | tf_op jit(solution)/shard_map/while/body/eval_jaxpr/ppermute | solution.py:16
  369.9 9.8 %collective-permute-start = (bf16[512,256]{1,0:T(8,128)(2,1)S(1)}, bf16[512,256]{1,0:T(8,128)(2,1)S(1)}, u32[]{:S(2)}, u32[]{:S(2)}) collective-permute-start(bf16[512,256]{1,0:T(8,128)(2,1)S(1)} %get-tuple-element.707), channel_id=1, source_target_pairs={{0,8},{8,16},{16,24},{24,32},{32,40},{40,48},{48,56},{56,64},{64,7... | collective-permute-start | bytes 786440 | tf_op jit(solution)/shard_map/while/body/eval_jaxpr/ppermute | solution.py:16
  379.7 12.5 %collective-permute-start = (bf16[512,256]{1,0:T(8,128)(2,1)S(1)}, bf16[512,256]{1,0:T(8,128)(2,1)S(1)}, u32[]{:S(2)}, u32[]{:S(2)}) collective-permute-start(bf16[512,256]{1,0:T(8,128)(2,1)S(1)} %get-tuple-element.707), channel_id=1, source_target_pairs={{0,8},{8,16},{16,24},{24,32},{32,40},{40,48},{48,56},{56,64},{64,7... | collective-permute-start | bytes 786440 | tf_op jit(solution)/shard_map/while/body/eval_jaxpr/ppermute | solution.py:16
  (19 other events, 662.7 us)
Sparse Core Ops, SparseCore 0:
  16.1 37.5 all-gather.1
  60.8 32.7 reduce-scatter.2
  402.6 101.9 reduce-scatter.4
where the time goes:
time: 514 us; the launch traced here: 513 us
  waiting for transfers between devices  273 us (53%)
  starting transfers between devices  173 us (34%)
  blocking collectives  20 us (4%)
  between operations  13.3 us (3%)
  other arithmetic  13.2 us (3%)
  matrix products  10.6 us (2%)
  local copies, waits for them, and re-layouts  8.94 us (2%)
    ppermute x31, starting transfers between devices, from_behind(): return lax.ppermute(block, axis, route)  173 us
    reduce_scatter x1, waiting for transfers between devices, per_device(): lax.psum_scatter(partial_terms.astype(jnp.bfloat16), 'tc', scatter_dimens...  102 us
    ppermute x31, waiting for transfers between devices, from_behind(): return lax.ppermute(block, axis, route)  102 us
    all_gather x1, waiting for transfers between devices, per_device(): normalized_rows = lax.all_gather(normed_local, 'tc', axis=0, tiled=True)  37.7 us
    reduce_scatter x1, waiting for transfers between devices, per_device(): lax.psum_scatter(jnp.concatenate([jnp.dot(normalized_rows, q_weight, pref...  31.2 us
  transfers between devices with their start and end apart: 34, of which 34 were waited for; matrix products, arithmetic and copies ran while one was open for 0% of the time, Pallas kernels for 0%

commit v1 on v0

--- a/solution.py
+++ b/solution.py
@@ -8,6 +8,27 @@
 epsilon = 1e-05
 rope_base = 500000.0
 masked_score = -1e30
+
+
+def gather_around(shard, axis, dim):
+    peers, place, width = (lax.axis_size(axis), lax.axis_index(axis), shard.shape[dim])
+    ahead = [(i, (i + 1) % peers) for i in range(peers)]
+    left = [(i, (i - 1) % peers) for i in range(peers)]
+    result = jnp.zeros((*shard.shape[:dim], peers * width, *shard.shape[dim + 1 :]), shard.dtype)
+    result = lax.dynamic_update_slice_in_dim(result, shard, place * width, axis=dim)
+    from_left = from_right = shard
+    middle = peers // 2
+    for step in range(1, middle + 1):
+        from_left = lax.ppermute(from_left, axis, ahead)
+        result = lax.dynamic_update_slice_in_dim(
+            result, from_left, (place - step) % peers * width, axis=dim
+        )
+        if step < peers - middle:
+            from_right = lax.ppermute(from_right, axis, left)
+            result = lax.dynamic_update_slice_in_dim(
+                result, from_right, (place + step) % peers * width, axis=dim
+            )
+    return result
 
 
 def from_behind(block, axis, distance):
@@ -42,7 +63,7 @@
     normed_local = (wide_hidden * lax.rsqrt(squares[:, None] / D + epsilon) * norm_gain).astype(
         jnp.bfloat16
     )
-    normalized_rows = lax.all_gather(normed_local, "tc", axis=0, tiled=True)
+    normalized_rows = gather_around(normed_local, "tc", 0)
     rows_per_block = normalized_rows.shape[0]
     query_rows = rows_per_block // lax.axis_size("tr")
     query_width = q_weight.shape[1]

time: 514 us -> 583 us (1.13)
  starting transfers between devices: 173 us -> 201 us
  local copies, waits for them, and re-layouts: 8.94 us -> 35.8 us
  waiting for transfers between devices: 273 us -> 283 us
    all_gather x1 -> x0, waiting for transfers between devices: 37.7 us -> none  [per_device(): normalized_rows = lax.all_gather(normed_local, 'tc', axis=0, tiled=True)]
    ppermute x31, starting transfers between devices: 173 us -> 196 us  [from_behind(): return lax.ppermute(block, axis, route)]
    while x31, local copies, waits for them, and re-layouts: 0.56 us -> 21.8 us
    reduce_scatter x1, waiting for transfers between devices: 102 us -> 118 us  [per_device(): lax.psum_scatter(partial_terms.astype(jnp.bfloat16), 'tc', scatter_dimens...]
    ppermute x0 -> x3, waiting for transfers between devices: none -> 15.4 us  [the longest x2 15.4 us: gather_around(): from_left = lax.ppermute(from_left, axis, ahead)]
    ppermute x31, waiting for transfers between devices: 102 us -> 112 us  [from_behind(): return lax.ppermute(block, axis, route)]
    reduce_scatter x1, waiting for transfers between devices: 31.2 us -> 37.9 us  [per_device(): lax.psum_scatter(jnp.concatenate([jnp.dot(normalized_rows, q_weight, pref...]
  transfers between devices with their start and end apart: 34 -> 36, of which waited for: 34 -> 35; matrix products, arithmetic and copies ran while one was open for 0% -> 1% of each run, Pallas kernels for 0% -> 0%
where the time goes in v1:
time: 583 us; the launch traced here: 580 us
  waiting for transfers between devices  283 us (49%)
  starting transfers between devices  201 us (34%)
  local copies, waits for them, and re-layouts  35.8 us (6%)
  blocking collectives  20.2 us (3%)
  matrix products  15.7 us (3%)
  between operations  13.6 us (2%)
  other arithmetic  10.5 us (2%)
    ppermute x31, starting transfers between devices, from_behind(): return lax.ppermute(block, axis, route)  196 us
    reduce_scatter x1, waiting for transfers between devices, per_device(): lax.psum_scatter(partial_terms.astype(jnp.bfloat16), 'tc', scatter_dimens...  118 us
    ppermute x31, waiting for transfers between devices, from_behind(): return lax.ppermute(block, axis, route)  112 us
    reduce_scatter x1, waiting for transfers between devices, per_device(): lax.psum_scatter(jnp.concatenate([jnp.dot(normalized_rows, q_weight, pref...  37.9 us
    while x31, local copies, waits for them, and re-layouts  21.8 us
    ppermute x2, waiting for transfers between devices, gather_around(): from_left = lax.ppermute(from_left, axis, ahead)  15.4 us
  transfers between devices with their start and end apart: 36, of which 35 were waited for; matrix products, arithmetic and copies ran while one was open for 1% of the time, Pallas kernels for 0%

profile of v1, /device:TPU:1, one launch (start us, length us, event | category | flops | bytes accessed | tf_op | source)
XLA Modules:
  0.0 579.9 jit_solution(14256449168230140061)
XLA Ops:
  7.9 6.0 %psum.7 = f32[128]{0:T(128)S(1)} all-reduce(f32[128]{0:T(128)S(1)} %fusion.40), channel_id=1, replica_groups=mesh['ctx'=32,'tr'=2,'tc'=4] {'tr'}, use_global_device_ids=true, to_apply=%region_1.0 | all-reduce | flops 128 | bytes 1024 | tf_op jit(solution)/shard_map/psum | solution.py:62
  19.4 8.5 %collective-permute-done.1 = bf16[128,2048]{1,0:T(8,128)(2,1)S(1)} collective-permute-done((bf16[128,2048]{1,0:T(8,128)(2,1)}, bf16[128,2048]{1,0:T(8,128)(2,1)S(1)}, u32[]{:S(2)}, u32[]{:S(2)}) %collective-permute-start.1) | collective-permute-done | bytes 524320 | tf_op jit(solution)/shard_map/ppermute | solution.py:22
  32.5 6.8 %collective-permute-done.3 = bf16[128,2048]{1,0:T(8,128)(2,1)} collective-permute-done((bf16[128,2048]{1,0:T(8,128)(2,1)S(1)}, bf16[128,2048]{1,0:T(8,128)(2,1)}, u32[]{:S(2)}, u32[]{:S(2)}) %collective-permute-start.3) | collective-permute-done | bytes 524320 | tf_op jit(solution)/shard_map/ppermute | solution.py:22
  51.6 37.9 %reduce-scatter.3.cloned.1.call-done = f32[256,768]{0,1:T(8,128)} async-done(((f32[512,768]{0,1:T(8,128)}), f32[256,768]{0,1:T(8,128)}) %reduce-scatter.3.cloned.1.call-update) | async-done | bytes 786448 | tf_op jit(solution)/shard_map/reduce_scatter | solution.py:71
  94.8 6.7 %all_gather.6 = bf16[512,256]{0,1:T(8,128)(2,1)S(1)} all-gather(bf16[256,256]{0,1:T(8,128)(2,1)S(1)} %pad_maximum_fusion.2), channel_id=1, replica_groups=mesh['ctx'=32,'tr'=2,'tc'=4] {'tr'}, dimensions={0}, use_global_device_ids=true | all-gather | bytes 393216 | tf_op jit(solution)/shard_map/all_gather | solution.py:150
  107.4 334.9 %while.22 = (s32[]{:T(128)}, bf16[512,256]{1,0:T(8,128)(2,1)}, f32[1,4,256]{2,1,0:T(4,128)S(1)}, f32[1,4,256]{2,1,0:T(4,128)S(1)}, f32[1,4,256,128]{3,2,1,0:T(8,...) while((s32[]{:T(128)}, bf16[512,256]{1,0:T(8,128)(2,1)}, ...), condition=%wide.region_18.19_spmd.clone, body=%wide.region_11.18_spmd.clone.sunk | while | flops 276142272 | bytes 10047672 | solution.py:158
  128.4 8.7 %collective-permute-start = (bf16[512,256]{1,0:T(8,128)(2,1)}, bf16[512,256]{1,0:T(8,128)(2,1)S(1)}, u32[]{:S(2)}, u32[]{:S(2)}) collective-permute-start(bf16[512,256]{1,0:T(8,128)(2,1)} %get-tuple-element.709), channel_id=1, source_target_pairs={{0,8},{8,16},{16,24},{24,32},{32,40},{40,48},{48,56},{56,64},{64,7... | collective-permute-start | bytes 786440 | tf_op jit(solution)/shard_map/while/body/eval_jaxpr/ppermute | solution.py:37
  150.0 6.0 %collective-permute-start = (bf16[512,256]{1,0:T(8,128)(2,1)}, bf16[512,256]{1,0:T(8,128)(2,1)S(1)}, u32[]{:S(2)}, u32[]{:S(2)}) collective-permute-start(bf16[512,256]{1,0:T(8,128)(2,1)} %get-tuple-element.709), channel_id=1, source_target_pairs={{0,8},{8,16},{16,24},{24,32},{32,40},{40,48},{48,56},{56,64},{64,7... | collective-permute-start | bytes 786440 | tf_op jit(solution)/shard_map/while/body/eval_jaxpr/ppermute | solution.py:37
  160.4 5.2 collective-permute-start
  169.9 9.6 %collective-permute-start = (bf16[512,256]{1,0:T(8,128)(2,1)}, bf16[512,256]{1,0:T(8,128)(2,1)S(1)}, u32[]{:S(2)}, u32[]{:S(2)}) collective-permute-start(bf16[512,256]{1,0:T(8,128)(2,1)} %get-tuple-element.709), channel_id=1, source_target_pairs={{0,8},{8,16},{16,24},{24,32},{32,40},{40,48},{48,56},{56,64},{64,7... | collective-permute-start | bytes 786440 | tf_op jit(solution)/shard_map/while/body/eval_jaxpr/ppermute | solution.py:37
  183.8 5.2 collective-permute-start
  193.3 5.2 collective-permute-start
  202.8 5.2 collective-permute-start
  250.3 8.5 %collective-permute-start = (bf16[512,256]{1,0:T(8,128)(2,1)}, bf16[512,256]{1,0:T(8,128)(2,1)S(1)}, u32[]{:S(2)}, u32[]{:S(2)}) collective-permute-start(bf16[512,256]{1,0:T(8,128)(2,1)} %get-tuple-element.709), channel_id=1, source_target_pairs={{0,8},{8,16},{16,24},{24,32},{32,40},{40,48},{48,56},{56,64},{64,7... | collective-permute-start | bytes 786440 | tf_op jit(solution)/shard_map/while/body/eval_jaxpr/ppermute | solution.py:37
  329.6 8.5 %collective-permute-start = (bf16[512,256]{1,0:T(8,128)(2,1)}, bf16[512,256]{1,0:T(8,128)(2,1)S(1)}, u32[]{:S(2)}, u32[]{:S(2)}) collective-permute-start(bf16[512,256]{1,0:T(8,128)(2,1)} %get-tuple-element.709), channel_id=1, source_target_pairs={{0,8},{8,16},{16,24},{24,32},{32,40},{40,48},{48,56},{56,64},{64,7... | collective-permute-start | bytes 786440 | tf_op jit(solution)/shard_map/while/body/eval_jaxpr/ppermute | solution.py:37
  351.9 8.5 %collective-permute-start = (bf16[512,256]{1,0:T(8,128)(2,1)}, bf16[512,256]{1,0:T(8,128)(2,1)S(1)}, u32[]{:S(2)}, u32[]{:S(2)}) collective-permute-start(bf16[512,256]{1,0:T(8,128)(2,1)} %get-tuple-element.709), channel_id=1, source_target_pairs={{0,8},{8,16},{16,24},{24,32},{32,40},{40,48},{48,56},{56,64},{64,7... | collective-permute-start | bytes 786440 | tf_op jit(solution)/shard_map/while/body/eval_jaxpr/ppermute | solution.py:37
  364.8 6.4 %collective-permute-start = (bf16[512,256]{1,0:T(8,128)(2,1)}, bf16[512,256]{1,0:T(8,128)(2,1)S(1)}, u32[]{:S(2)}, u32[]{:S(2)}) collective-permute-start(bf16[512,256]{1,0:T(8,128)(2,1)} %get-tuple-element.709), channel_id=1, source_target_pairs={{0,8},{8,16},{16,24},{24,32},{32,40},{40,48},{48,56},{56,64},{64,7... | collective-permute-start | bytes 786440 | tf_op jit(solution)/shard_map/while/body/eval_jaxpr/ppermute | solution.py:37
  375.5 10.8 %collective-permute-start = (bf16[512,256]{1,0:T(8,128)(2,1)}, bf16[512,256]{1,0:T(8,128)(2,1)S(1)}, u32[]{:S(2)}, u32[]{:S(2)}) collective-permute-start(bf16[512,256]{1,0:T(8,128)(2,1)} %get-tuple-element.709), channel_id=1, source_target_pairs={{0,8},{8,16},{16,24},{24,32},{32,40},{40,48},{48,56},{56,64},{64,7... | collective-permute-start | bytes 786440 | tf_op jit(solution)/shard_map/while/body/eval_jaxpr/ppermute | solution.py:37
  390.6 6.4 %collective-permute-start = (bf16[512,256]{1,0:T(8,128)(2,1)}, bf16[512,256]{1,0:T(8,128)(2,1)S(1)}, u32[]{:S(2)}, u32[]{:S(2)}) collective-permute-start(bf16[512,256]{1,0:T(8,128)(2,1)} %get-tuple-element.709), channel_id=1, source_target_pairs={{0,8},{8,16},{16,24},{24,32},{32,40},{40,48},{48,56},{56,64},{64,7... | collective-permute-start | bytes 786440 | tf_op jit(solution)/shard_map/while/body/eval_jaxpr/ppermute | solution.py:37
  401.3 10.8 %collective-permute-start = (bf16[512,256]{1,0:T(8,128)(2,1)}, bf16[512,256]{1,0:T(8,128)(2,1)S(1)}, u32[]{:S(2)}, u32[]{:S(2)}) collective-permute-start(bf16[512,256]{1,0:T(8,128)(2,1)} %get-tuple-element.709), channel_id=1, source_target_pairs={{0,8},{8,16},{16,24},{24,32},{32,40},{40,48},{48,56},{56,64},{64,7... | collective-permute-start | bytes 786440 | tf_op jit(solution)/shard_map/while/body/eval_jaxpr/ppermute | solution.py:37
  416.4 6.4 %collective-permute-start = (bf16[512,256]{1,0:T(8,128)(2,1)}, bf16[512,256]{1,0:T(8,128)(2,1)S(1)}, u32[]{:S(2)}, u32[]{:S(2)}) collective-permute-start(bf16[512,256]{1,0:T(8,128)(2,1)} %get-tuple-element.709), channel_id=1, source_target_pairs={{0,8},{8,16},{16,24},{24,32},{32,40},{40,48},{48,56},{56,64},{64,7... | collective-permute-start | bytes 786440 | tf_op jit(solution)/shard_map/while/body/eval_jaxpr/ppermute | solution.py:37
  427.1 10.8 %collective-permute-start = (bf16[512,256]{1,0:T(8,128)(2,1)}, bf16[512,256]{1,0:T(8,128)(2,1)S(1)}, u32[]{:S(2)}, u32[]{:S(2)}) collective-permute-start(bf16[512,256]{1,0:T(8,128)(2,1)} %get-tuple-element.709), channel_id=1, source_target_pairs={{0,8},{8,16},{16,24},{24,32},{32,40},{40,48},{48,56},{56,64},{64,7... | collective-permute-start | bytes 786440 | tf_op jit(solution)/shard_map/while/body/eval_jaxpr/ppermute | solution.py:37
  443.6 7.4 %all_gather.7 = bf16[512,512]{0,1:T(8,128)(2,1)S(1)} all-gather(bf16[256,512]{0,1:T(8,128)(2,1)S(1)} %bitcast.110), channel_id=1, replica_groups=mesh['ctx'=32,'tr'=2,'tc'=4] {'tr'}, dimensions={0}, use_global_device_ids=true | all-gather | bytes 786432 | tf_op jit(solution)/shard_map/all_gather | solution.py:165
  453.6 117.5 %reduce-scatter.5.cloned.1.call-done = bf16[128,2048]{1,0:T(8,128)(2,1)} async-done(((bf16[512,2048]{1,0:T(8,128)(2,1)}), bf16[128,2048]{1,0:T(8,128)(2,1)}) %reduce-scatter.5.cloned.1.call-update) | async-done | bytes 524304 | tf_op jit(solution)/shard_map/reduce_scatter | solution.py:169
  (223 shorter events, 260.5 us)
Async XLA Ops:
  6.5 83.0 %reduce-scatter.3.cloned.1.call-start = ((), (), s32[]{:S(2)}) async-start(), calls=%async_computation.2 | async-start | bytes 2359296 | tf_op jit(solution)/shard_map/reduce_scatter | solution.py:71
  16.8 11.2 %collective-permute-start.1 = (bf16[128,2048]{1,0:T(8,128)(2,1)}, bf16[128,2048]{1,0:T(8,128)(2,1)S(1)}, u32[]{:S(2)}, u32[]{:S(2)}) collective-permute-start(bf16[128,2048]{1,0:T(8,128)(2,1)} %get-tuple-element.603), channel_id=1, source_target_pairs={{0,1},{1,2},{2,3},{3,0},{4,5},{5,6},{6,7},{7,4},{8,9},{9,10},{10,1... | collective-permute-start | bytes 1572872 | tf_op jit(solution)/shard_map/ppermute | solution.py:22
  18.1 12.5 %collective-permute-start.2 = (bf16[128,2048]{1,0:T(8,128)(2,1)}, bf16[128,2048]{1,0:T(8,128)(2,1)}, u32[]{:S(2)}, u32[]{:S(2)}) collective-permute-start(bf16[128,2048]{1,0:T(8,128)(2,1)} %get-tuple-element.603), channel_id=1, source_target_pairs={{0,3},{1,0},{2,1},{3,2},{4,7},{5,4},{6,5},{7,6},{8,11},{9,8},{10,9... | collective-permute-start | bytes 1572872 | tf_op jit(solution)/shard_map/ppermute | solution.py:27
  28.0 11.4 %collective-permute-start.3 = (bf16[128,2048]{1,0:T(8,128)(2,1)S(1)}, bf16[128,2048]{1,0:T(8,128)(2,1)}, u32[]{:S(2)}, u32[]{:S(2)}) collective-permute-start(bf16[128,2048]{1,0:T(8,128)(2,1)S(1)} %collective-permute-done.1), channel_id=1, source_target_pairs={{0,1},{1,2},{2,3},{3,0},{4,5},{5,6},{6,7},{7,4},{8,9},{9,10},{10,1... | collective-permute-start | bytes 1572872 | tf_op jit(solution)/shard_map/ppermute | solution.py:22
  50.5 520.6 %reduce-scatter.5.cloned.1.call-start = ((), (), s32[]{:S(2)}) async-start(), calls=%async_computation.3 | async-start | bytes 2621440 | tf_op jit(solution)/shard_map/reduce_scatter | solution.py:169
  128.4 12.3 %collective-permute-start = (bf16[512,256]{1,0:T(8,128)(2,1)}, bf16[512,256]{1,0:T(8,128)(2,1)S(1)}, u32[]{:S(2)}, u32[]{:S(2)}) collective-permute-start(bf16[512,256]{1,0:T(8,128)(2,1)} %get-tuple-element.709), channel_id=1, source_target_pairs={{0,8},{8,16},{16,24},{24,32},{32,40},{40,48},{48,56},{56,64},{64,7... | collective-permute-start | bytes 786440 | tf_op jit(solution)/shard_map/while/body/eval_jaxpr/ppermute | solution.py:37
  150.0 9.6 %collective-permute-start = (bf16[512,256]{1,0:T(8,128)(2,1)}, bf16[512,256]{1,0:T(8,128)(2,1)S(1)}, u32[]{:S(2)}, u32[]{:S(2)}) collective-permute-start(bf16[512,256]{1,0:T(8,128)(2,1)} %get-tuple-element.709), channel_id=1, source_target_pairs={{0,8},{8,16},{16,24},{24,32},{32,40},{40,48},{48,56},{56,64},{64,7... | collective-permute-start | bytes 786440 | tf_op jit(solution)/shard_map/while/body/eval_jaxpr/ppermute | solution.py:37
  160.4 8.8 %collective-permute-start = (bf16[512,256]{1,0:T(8,128)(2,1)}, bf16[512,256]{1,0:T(8,128)(2,1)S(1)}, u32[]{:S(2)}, u32[]{:S(2)}) collective-permute-start(bf16[512,256]{1,0:T(8,128)(2,1)} %get-tuple-element.709), channel_id=1, source_target_pairs={{0,8},{8,16},{16,24},{24,32},{32,40},{40,48},{48,56},{56,64},{64,7... | collective-permute-start | bytes 786440 | tf_op jit(solution)/shard_map/while/body/eval_jaxpr/ppermute | solution.py:37
  169.9 13.2 %collective-permute-start = (bf16[512,256]{1,0:T(8,128)(2,1)}, bf16[512,256]{1,0:T(8,128)(2,1)S(1)}, u32[]{:S(2)}, u32[]{:S(2)}) collective-permute-start(bf16[512,256]{1,0:T(8,128)(2,1)} %get-tuple-element.709), channel_id=1, source_target_pairs={{0,8},{8,16},{16,24},{24,32},{32,40},{40,48},{48,56},{56,64},{64,7... | collective-permute-start | bytes 786440 | tf_op jit(solution)/shard_map/while/body/eval_jaxpr/ppermute | solution.py:37
  183.8 8.8 %collective-permute-start = (bf16[512,256]{1,0:T(8,128)(2,1)}, bf16[512,256]{1,0:T(8,128)(2,1)S(1)}, u32[]{:S(2)}, u32[]{:S(2)}) collective-permute-start(bf16[512,256]{1,0:T(8,128)(2,1)} %get-tuple-element.709), channel_id=1, source_target_pairs={{0,8},{8,16},{16,24},{24,32},{32,40},{40,48},{48,56},{56,64},{64,7... | collective-permute-start | bytes 786440 | tf_op jit(solution)/shard_map/while/body/eval_jaxpr/ppermute | solution.py:37
  193.3 8.8 %collective-permute-start = (bf16[512,256]{1,0:T(8,128)(2,1)}, bf16[512,256]{1,0:T(8,128)(2,1)S(1)}, u32[]{:S(2)}, u32[]{:S(2)}) collective-permute-start(bf16[512,256]{1,0:T(8,128)(2,1)} %get-tuple-element.709), channel_id=1, source_target_pairs={{0,8},{8,16},{16,24},{24,32},{32,40},{40,48},{48,56},{56,64},{64,7... | collective-permute-start | bytes 786440 | tf_op jit(solution)/shard_map/while/body/eval_jaxpr/ppermute | solution.py:37
  202.8 8.8 %collective-permute-start = (bf16[512,256]{1,0:T(8,128)(2,1)}, bf16[512,256]{1,0:T(8,128)(2,1)S(1)}, u32[]{:S(2)}, u32[]{:S(2)}) collective-permute-start(bf16[512,256]{1,0:T(8,128)(2,1)} %get-tuple-element.709), channel_id=1, source_target_pairs={{0,8},{8,16},{16,24},{24,32},{32,40},{40,48},{48,56},{56,64},{64,7... | collective-permute-start | bytes 786440 | tf_op jit(solution)/shard_map/while/body/eval_jaxpr/ppermute | solution.py:37
  212.3 8.8 %collective-permute-start = (bf16[512,256]{1,0:T(8,128)(2,1)}, bf16[512,256]{1,0:T(8,128)(2,1)S(1)}, u32[]{:S(2)}, u32[]{:S(2)}) collective-permute-start(bf16[512,256]{1,0:T(8,128)(2,1)} %get-tuple-element.709), channel_id=1, source_target_pairs={{0,8},{8,16},{16,24},{24,32},{32,40},{40,48},{48,56},{56,64},{64,7... | collective-permute-start | bytes 786440 | tf_op jit(solution)/shard_map/while/body/eval_jaxpr/ppermute | solution.py:37
  221.8 8.8 %collective-permute-start = (bf16[512,256]{1,0:T(8,128)(2,1)}, bf16[512,256]{1,0:T(8,128)(2,1)S(1)}, u32[]{:S(2)}, u32[]{:S(2)}) collective-permute-start(bf16[512,256]{1,0:T(8,128)(2,1)} %get-tuple-element.709), channel_id=1, source_target_pairs={{0,8},{8,16},{16,24},{24,32},{32,40},{40,48},{48,56},{56,64},{64,7... | collective-permute-start | bytes 786440 | tf_op jit(solution)/shard_map/while/body/eval_jaxpr/ppermute | solution.py:37
  250.3 12.1 %collective-permute-start = (bf16[512,256]{1,0:T(8,128)(2,1)}, bf16[512,256]{1,0:T(8,128)(2,1)S(1)}, u32[]{:S(2)}, u32[]{:S(2)}) collective-permute-start(bf16[512,256]{1,0:T(8,128)(2,1)} %get-tuple-element.709), channel_id=1, source_target_pairs={{0,8},{8,16},{16,24},{24,32},{32,40},{40,48},{48,56},{56,64},{64,7... | collective-permute-start | bytes 786440 | tf_op jit(solution)/shard_map/while/body/eval_jaxpr/ppermute | solution.py:37
  263.1 8.8 %collective-permute-start = (bf16[512,256]{1,0:T(8,128)(2,1)}, bf16[512,256]{1,0:T(8,128)(2,1)S(1)}, u32[]{:S(2)}, u32[]{:S(2)}) collective-permute-start(bf16[512,256]{1,0:T(8,128)(2,1)} %get-tuple-element.709), channel_id=1, source_target_pairs={{0,8},{8,16},{16,24},{24,32},{32,40},{40,48},{48,56},{56,64},{64,7... | collective-permute-start | bytes 786440 | tf_op jit(solution)/shard_map/while/body/eval_jaxpr/ppermute | solution.py:37
  329.6 12.1 %collective-permute-start = (bf16[512,256]{1,0:T(8,128)(2,1)}, bf16[512,256]{1,0:T(8,128)(2,1)S(1)}, u32[]{:S(2)}, u32[]{:S(2)}) collective-permute-start(bf16[512,256]{1,0:T(8,128)(2,1)} %get-tuple-element.709), channel_id=1, source_target_pairs={{0,8},{8,16},{16,24},{24,32},{32,40},{40,48},{48,56},{56,64},{64,7... | collective-permute-start | bytes 786440 | tf_op jit(solution)/shard_map/while/body/eval_jaxpr/ppermute | solution.py:37
  351.9 12.2 %collective-permute-start = (bf16[512,256]{1,0:T(8,128)(2,1)}, bf16[512,256]{1,0:T(8,128)(2,1)S(1)}, u32[]{:S(2)}, u32[]{:S(2)}) collective-permute-start(bf16[512,256]{1,0:T(8,128)(2,1)} %get-tuple-element.709), channel_id=1, source_target_pairs={{0,8},{8,16},{16,24},{24,32},{32,40},{40,48},{48,56},{56,64},{64,7... | collective-permute-start | bytes 786440 | tf_op jit(solution)/shard_map/while/body/eval_jaxpr/ppermute | solution.py:37
  364.8 10.0 %collective-permute-start = (bf16[512,256]{1,0:T(8,128)(2,1)}, bf16[512,256]{1,0:T(8,128)(2,1)S(1)}, u32[]{:S(2)}, u32[]{:S(2)}) collective-permute-start(bf16[512,256]{1,0:T(8,128)(2,1)} %get-tuple-element.709), channel_id=1, source_target_pairs={{0,8},{8,16},{16,24},{24,32},{32,40},{40,48},{48,56},{56,64},{64,7... | collective-permute-start | bytes 786440 | tf_op jit(solution)/shard_map/while/body/eval_jaxpr/ppermute | solution.py:37
  375.5 14.4 %collective-permute-start = (bf16[512,256]{1,0:T(8,128)(2,1)}, bf16[512,256]{1,0:T(8,128)(2,1)S(1)}, u32[]{:S(2)}, u32[]{:S(2)}) collective-permute-start(bf16[512,256]{1,0:T(8,128)(2,1)} %get-tuple-element.709), channel_id=1, source_target_pairs={{0,8},{8,16},{16,24},{24,32},{32,40},{40,48},{48,56},{56,64},{64,7... | collective-permute-start | bytes 786440 | tf_op jit(solution)/shard_map/while/body/eval_jaxpr/ppermute | solution.py:37
  390.6 10.0 %collective-permute-start = (bf16[512,256]{1,0:T(8,128)(2,1)}, bf16[512,256]{1,0:T(8,128)(2,1)S(1)}, u32[]{:S(2)}, u32[]{:S(2)}) collective-permute-start(bf16[512,256]{1,0:T(8,128)(2,1)} %get-tuple-element.709), channel_id=1, source_target_pairs={{0,8},{8,16},{16,24},{24,32},{32,40},{40,48},{48,56},{56,64},{64,7... | collective-permute-start | bytes 786440 | tf_op jit(solution)/shard_map/while/body/eval_jaxpr/ppermute | solution.py:37
  401.3 14.4 %collective-permute-start = (bf16[512,256]{1,0:T(8,128)(2,1)}, bf16[512,256]{1,0:T(8,128)(2,1)S(1)}, u32[]{:S(2)}, u32[]{:S(2)}) collective-permute-start(bf16[512,256]{1,0:T(8,128)(2,1)} %get-tuple-element.709), channel_id=1, source_target_pairs={{0,8},{8,16},{16,24},{24,32},{32,40},{40,48},{48,56},{56,64},{64,7... | collective-permute-start | bytes 786440 | tf_op jit(solution)/shard_map/while/body/eval_jaxpr/ppermute | solution.py:37
  416.4 10.0 %collective-permute-start = (bf16[512,256]{1,0:T(8,128)(2,1)}, bf16[512,256]{1,0:T(8,128)(2,1)S(1)}, u32[]{:S(2)}, u32[]{:S(2)}) collective-permute-start(bf16[512,256]{1,0:T(8,128)(2,1)} %get-tuple-element.709), channel_id=1, source_target_pairs={{0,8},{8,16},{16,24},{24,32},{32,40},{40,48},{48,56},{56,64},{64,7... | collective-permute-start | bytes 786440 | tf_op jit(solution)/shard_map/while/body/eval_jaxpr/ppermute | solution.py:37
  427.1 14.4 %collective-permute-start = (bf16[512,256]{1,0:T(8,128)(2,1)}, bf16[512,256]{1,0:T(8,128)(2,1)S(1)}, u32[]{:S(2)}, u32[]{:S(2)}) collective-permute-start(bf16[512,256]{1,0:T(8,128)(2,1)} %get-tuple-element.709), channel_id=1, source_target_pairs={{0,8},{8,16},{16,24},{24,32},{32,40},{40,48},{48,56},{56,64},{64,7... | collective-permute-start | bytes 786440 | tf_op jit(solution)/shard_map/while/body/eval_jaxpr/ppermute | solution.py:37
  (19 other events, 583.1 us)
Sparse Core Ops, SparseCore 0:
  50.7 38.8 reduce-scatter.2
  453.8 117.3 reduce-scatter.4
